TPU v7x, 512 devices: a whole 4x8x8 slice. The times are simulated.
512 devices in a mesh: cfg: 2 (over y_lo), patch: 64 (over z, x, core), rep: 4 (over y_hi).
Axes of the slice: x: 4, y: 8 (y_hi: 4, y_lo: 2; y = y_hi * 2 + y_lo), z: 8, core: 2. Of those that a mesh axis runs over, the one named last changes fastest.
Arguments:
- queries: bfloat16 [2, 2560, 6144], P('cfg', 'patch', 'rep'), parts along dimension 2, may hold values from -8 to 8
- fresh_keys: bfloat16 [2, 2560, 6144], P('cfg', 'patch', 'rep'), parts along dimension 2, may hold values from -8 to 8
- fresh_values: bfloat16 [2, 2560, 6144], P('cfg', 'patch', 'rep'), parts along dimension 2, may hold values from -6 to 6
- stale_keys: bfloat16 [2, 2560, 6144], P('cfg', 'patch', 'rep'), parts along dimension 2, may hold values from -6 to 6
- stale_values: bfloat16 [2, 2560, 6144], P('cfg', 'patch', 'rep'), parts along dimension 2, may hold values from -6 to 6
- text_keys: bfloat16 [2, 1024, 1536], P('cfg', 'rep'), parts along dimension 1, may hold values from -8 to 8
- text_values: bfloat16 [2, 1024, 1536], P('cfg', 'rep'), parts along dimension 1, may hold values from -6 to 6
- text_count: int32 [2], P('cfg'), may hold values from 64 to 256, as said below
- positions: int32 [12, 2560], P('rep', 'patch'), parts along dimension 0, may hold values from 0 to 15, as said below
- mod_shift: float32 [2, 1536], P('cfg'), may hold values from -3 to 3
- mod_scale: float32 [2, 1536], P('cfg'), may hold values from -1.5 to 1.5
- proj_out: bfloat16 [1536, 64], replicated, may hold values from -0.15625 to 0.15625
Outputs:
- guided: float32 [2, 2560, 128], P('cfg', 'patch', 'rep'), parts along dimension 2
There are 4 independent parts, one for each index of `rep`. A program takes and returns all parts, laid end to end along the dimension named above; an argument that names none is the same for every part. Nothing has to cross between parts.
Inputs may be any that keep to these rules, and one draw needn't show every extreme that they name: `positions`: each token has its own cell in a video of 16 x 16 cells a frame, numbered in raster order; the 40 tokens of one device are consecutive cells. `text_count`: one of the two branches has all 256 text tokens live, the other fewer.
All inputs are finite; a program needn't handle non-finite values.
Results may differ from a plain program's by a relative error of at most 0.009.
Values may be sent and summed in bfloat16 or wider, within the bound.
A program may use at most 128 MiB of HBM per device.

v0:
```python
import math

import jax
import jax.numpy as jnp
from jax import lax
from jax.sharding import PartitionSpec as P

HEADS = 12
HEAD_DIM = 128


GUIDANCE = 4.0
EPSILON = 1e-06


def partner_2(shard, axis, stride):
    return lax.ppermute(shard, axis, [(i, i ^ 1 << stride) for i in range(lax.axis_size(axis))])


def rope_angles(positions, head_dim):
    time_extent = head_dim // 8
    space_extent = (head_dim - time_extent) // 2
    pieces = []
    for axis_number, extent in ((0, time_extent), (1, space_extent), (2, space_extent)):
        frequency = 256.0 ** (-jnp.arange(0, extent, 2).astype(jnp.float32) / extent)
        pieces.append(positions[axis_number].astype(jnp.float32)[:, None] * frequency[None, :])
    return jnp.concatenate(pieces, axis=1)


def rotate(values, angles):
    pairs = values.reshape(values.shape[0], values.shape[1], values.shape[2] // 2, 2)
    cosine = jnp.cos(angles)[:, None, :]
    sine_part = jnp.sin(angles)[:, None, :]
    first = pairs[..., 0]
    second = pairs[..., 1]
    turned = jnp.stack(
        [first * cosine - second * sine_part, first * sine_part + second * cosine], axis=-1
    )
    return turned.reshape(values.shape)


def absorb(carry, scores, values):
    top_old, total_old, accum_old = carry
    top_new = jnp.maximum(top_old, jnp.max(scores, axis=2))
    rescale = jnp.exp(top_old - top_new)
    weights = jnp.exp(scores - top_new[:, :, None])
    total_new = total_old * rescale + jnp.sum(weights, axis=2)
    accum_new = accum_old * rescale[:, :, None] + jnp.einsum(
        "hqk,khd->hqd", weights.astype(jnp.bfloat16), values, preferred_element_type=jnp.float32
    )
    return (top_new, total_new, accum_new)


def shards(
    queries,
    fresh_keys,
    fresh_values,
    stale_keys,
    stale_values,
    text_keys,
    text_values,
    text_count,
    positions,
    mod_shift,
    mod_scale,
    proj_out,
):
    rows = queries.shape[1]
    factor = 1.0 / math.sqrt(HEAD_DIM)
    angles = rope_angles(positions, HEAD_DIM)

    def split_heads(array):
        return array[0].reshape(array.shape[1], HEADS, HEAD_DIM)

    rot_queries = rotate(split_heads(queries).astype(jnp.float32), angles).astype(jnp.bfloat16)
    rot_keys = rotate(split_heads(fresh_keys).astype(jnp.float32), angles).astype(jnp.bfloat16)
    own_values = split_heads(fresh_values)
    word_keys = split_heads(text_keys)
    word_values = split_heads(text_values)
    word_live = jnp.arange(word_keys.shape[0]) < text_count[0]

    def score(keys):
        return (
            jnp.einsum("qhd,khd->hqk", rot_queries, keys, preferred_element_type=jnp.float32)
            * factor
        )

    device_number = lax.axis_index("patch")
    blank = (
        jnp.full((HEADS, rows), -1e30, jnp.float32),
        jnp.zeros((HEADS, rows), jnp.float32),
        jnp.zeros((HEADS, rows, HEAD_DIM), jnp.float32),
    )
    carry = blank
    carry = absorb(carry, score(rot_keys), own_values)
    word_scores = jnp.where(word_live[None, None, :], score(word_keys), -jnp.inf)
    initial = absorb(carry, word_scores, word_values)
    piece = (
        lax.all_gather(stale_keys, "patch", axis=1, tiled=True),
        lax.all_gather(stale_values, "patch", axis=1, tiled=True),
    )
    keys = piece[0][0].reshape(piece[0].shape[1], HEADS, HEAD_DIM)
    values = piece[1][0].reshape(piece[1].shape[1], HEADS, HEAD_DIM)
    key_index = jnp.arange(keys.shape[0])
    foreign = key_index // rows != device_number
    carry = absorb(initial, jnp.where(foreign[None, None, :], score(keys), -jnp.inf), values)
    top_final, total_final, accum_final = carry
    attended = jnp.swapaxes(accum_final / total_final[:, :, None], 0, 1).reshape(
        rows, HEADS * HEAD_DIM
    )
    center = attended - jnp.mean(attended, axis=1, keepdims=True)
    normed = center * lax.rsqrt(jnp.mean(center * center, axis=1, keepdims=True) + EPSILON)
    modulated = (normed * (1.0 + mod_scale[0]) + mod_shift[0]).astype(jnp.bfloat16)
    predicted = jnp.dot(modulated, proj_out, preferred_element_type=jnp.float32)
    branch = lax.axis_index("cfg")
    own_weight = jnp.where(branch == 1, GUIDANCE, 1.0 - GUIDANCE)
    half_width = predicted.shape[1] // 2
    partner = partner_2(predicted, "cfg", 0)
    other_weight = jnp.where(branch == 1, 1.0 - GUIDANCE, GUIDANCE)
    combined = own_weight * predicted + other_weight * partner
    guided = lax.dynamic_slice_in_dim(combined, branch * half_width, half_width, 1)
    return guided[None]


def solution(mesh):
    placed = (
        P("cfg", "patch", "rep"),
        P("cfg", "patch", "rep"),
        P("cfg", "patch", "rep"),
        P("cfg", "patch", "rep"),
        P("cfg", "patch", "rep"),
        P("cfg", "rep", None),
        P("cfg", "rep", None),
        P("cfg"),
        P("rep", "patch"),
        P("cfg", None),
        P("cfg", None),
        P(),
    )
    return jax.shard_map(
        shards, mesh=mesh, in_specs=placed, out_specs=P("cfg", "patch", "rep"), check_vma=False
    )
```

profile of v0, /device:TPU:1, one launch (start us, length us, event | category | flops | bytes accessed | tf_op | source)
XLA Modules:
  0.0 224.3 jit_solution(16791111103496469696)
XLA Ops:
  6.6 0.7 all-gather.3.cloned.1.call-update
  7.3 0.7 all-gather.5.cloned.1.call-update
  8.0 1.1 copy.39
  9.1 1.1 copy.40
  10.2 1.4 copy.45
  12.2 1.7 reshape_squeeze.17
  13.9 1.4 copy.48
  15.8 2.2 subtract_convert_fusion
  18.0 1.0 pad_maximum_fusion
  19.0 1.0 pad_maximum_fusion.1
  20.0 0.3 fusion.57
  20.3 0.4 fusion.56
  20.7 84.2 %all-gather.3.cloned.1.call-done = bf16[1,2560,1536]{2,1,0:T(8,128)(2,1)} async-done(((bf16[1,40,1536]{2,1,0:T(8,128)(2,1)}), bf16[1,2560,1536]{2,1,0:T(8,128)(2,1)}) %all-gather.3.cloned.1.call-update) | async-done | bytes 7864336 | tf_op jit(solution)/shard_map/all_gather | solution.py:99
  104.9 10.4 %copy.50 = bf16[1,2560,1536]{1,2,0:T(8,128)(2,1)} copy(bf16[1,2560,1536]{2,1,0:T(8,128)(2,1)} %all-gather.3.cloned.1.call-done) | data formatting | bytes 15728640 | tf_op jit(solution)/shard_map/all_gather | solution.py:99
  115.3 4.8 %fusion.55 = (f32[12,40]{1,0:T(8,128)S(1)}, f32[12,40,2560]{2,1,0:T(8,128)S(1)}) fusion(bf16[40,12,128]{0,2,1:T(8,128)(2,1)S(1)} %bitcast.108, bf16[2560,12,128]{0,2,1:T(8,128)(2,1)} %bitcast.104, pred[2560]{0:T(1024)(128)(4,1)S(1)} %fusion.41), kind=kOutput, calls=%fused_computation.86 | convolution fusion | flops 318258720 | bytes 12906880 | tf_op jit(solution)/shard_map/qhd,khd->hqk/dot_general | solution.py:84
  120.4 1.8 copy-done.1
  122.2 0.8 fusion
  123.4 0.4 fusion.15
  123.8 69.7 %all-gather.5.cloned.1.call-done = bf16[1,2560,1536]{2,1,0:T(8,128)(2,1)} async-done(((bf16[1,40,1536]{2,1,0:T(8,128)(2,1)}), bf16[1,2560,1536]{2,1,0:T(8,128)(2,1)}) %all-gather.5.cloned.1.call-update) | async-done | bytes 7864336 | tf_op jit(solution)/shard_map/all_gather | solution.py:100
  193.5 10.4 %copy.53 = bf16[1,2560,1536]{1,2,0:T(8,128)(2,1)} copy(bf16[1,2560,1536]{2,1,0:T(8,128)(2,1)} %all-gather.5.cloned.1.call-done) | data formatting | bytes 15728640 | tf_op jit(solution)/shard_map/all_gather | solution.py:100
  203.9 7.7 %fusion.58 = (f32[40]{0:T(128)S(1)}, f32[40,12,128]{2,0,1:T(8,128)S(1)}) fusion(f32[40,12]{0,1:T(8,128)S(1)} %get-tuple-element.5, f32[40,12,128]{2,0,1:T(8,128)S(1)} %fusion.15, bf16[2560,12,128]{0,2,1:T(8,128)(2,1)} %bitcast.105, f32[12,40,2560]{2,1,0:T(8,128)} %copy-done.1, f32[12,40]{1,0:T(8,128)S(1)} %get-tuple-element.7), kind=kOutput, calls=%fused_computation.89 | convolution fusion | flops 317214688 | bytes 13275040 | tf_op jit(solution)/shard_map/hqk,khd->hqd/dot_general | solution.py:48
  212.1 3.1 %collective-permute-start = (f32[40,64]{1,0:T(8,128)S(1)}, f32[40,64]{1,0:T(8,128)S(1)}, u32[]{:S(2)}, u32[]{:S(2)}) collective-permute-start(f32[40,64]{1,0:T(8,128)S(1)} %fusion.30), channel_id=1, source_target_pairs={{0,256},{256,0},{1,257},{257,1},{2,258},{258,2},{3,259},{259,3},{4... | collective-permute-start | bytes 30728 | tf_op jit(solution)/shard_map/ppermute | solution.py:17
  215.3 1.4 collective-permute-done
  216.8 0.7 copy.56
  (33 shorter events, 1.6 us)
Async XLA Ops:
  6.5 205.3 %copy-start = (bf16[1536,64]{0,1:T(8,128)(2,1)S(1)}, bf16[1536,64]{0,1:T(8,128)(2,1)}, u32[]{:S(2)}) copy-start(bf16[1536,64]{0,1:T(8,128)(2,1)} %param.23) | copy-start | bytes 589828
  6.5 8.8 %copy-start.4 = (f32[1,1536]{1,0:T(1,128)S(1)}, f32[1,1536]{1,0:T(1,128)}, u32[]{:S(2)}) copy-start(f32[1,1536]{1,0:T(1,128)} %param.21) | copy-start | bytes 18436
  6.5 8.9 %copy-start.3 = (f32[1,1536]{1,0:T(1,128)S(1)}, f32[1,1536]{1,0:T(1,128)}, u32[]{:S(2)}) copy-start(f32[1,1536]{1,0:T(1,128)} %param.22) | copy-start | bytes 18436
  6.5 8.9 %copy-start.5 = (s32[3,40]{1,0:T(4,128)S(1)}, s32[3,40]{1,0:T(4,128)}, u32[]{:S(2)}) copy-start(s32[3,40]{1,0:T(4,128)} %param.20) | copy-start | bytes 1444
  6.5 98.3 %all-gather.3.cloned.1.call-start = ((), (), s32[]{:S(2)}) async-start(), calls=%async_computation | async-start | bytes 7987200 | tf_op jit(solution)/shard_map/all_gather | solution.py:99
  7.3 186.2 %all-gather.5.cloned.1.call-start = ((), (), s32[]{:S(2)}) async-start(), calls=%async_computation.1 | async-start | bytes 7987200 | tf_op jit(solution)/shard_map/all_gather | solution.py:100
  120.0 2.2 copy-start.1
  120.0 3.0 %copy-start.2 = (bf16[40,12,128]{2,1,0:T(8,128)(2,1)S(1)}, bf16[40,12,128]{2,1,0:T(8,128)(2,1)}, u32[]{:S(2)}) copy-start(bf16[40,12,128]{2,1,0:T(8,128)(2,1)} %reshape_squeeze.17) | copy-start | bytes 368644
  212.1 4.5 %collective-permute-start = (f32[40,64]{1,0:T(8,128)S(1)}, f32[40,64]{1,0:T(8,128)S(1)}, u32[]{:S(2)}, u32[]{:S(2)}) collective-permute-start(f32[40,64]{1,0:T(8,128)S(1)} %fusion.30), channel_id=1, source_target_pairs={{0,256},{256,0},{1,257},{257,1},{2,258},{258,2},{3,259},{259,3},{4... | collective-permute-start | bytes 30728 | tf_op jit(solution)/shard_map/ppermute | solution.py:17
Sparse Core Ops, SparseCore 0:
  10.7 94.1 all-gather.2
  108.2 85.2 all-gather.4
where the time goes:
time: 225 us; the launch traced here: 224 us
  waiting for transfers between devices  157 us (70%)
  local copies, waits for them, and re-layouts  30 us (13%)
  between operations  14.3 us (6%)
  matrix products  14.1 us (6%)
  other arithmetic  6.08 us (3%)
  starting transfers between devices  3.18 us (1%)
    all_gather x1, waiting for transfers between devices, shards(): lax.all_gather(stale_keys, 'patch', axis=1, tiled=True)  84.2 us
    all_gather x1, waiting for transfers between devices, shards(): lax.all_gather(stale_values, 'patch', axis=1, tiled=True)  69.7 us
    all_gather x1, local copies, waits for them, and re-layouts, shards(): lax.all_gather(stale_values, 'patch', axis=1, tiled=True)  10.4 us
    all_gather x1, local copies, waits for them, and re-layouts, shards(): lax.all_gather(stale_keys, 'patch', axis=1, tiled=True)  10.4 us
    dot_general x3, matrix products, absorb(): jnp.einsum('hqk,khd->hqd', weights.astype(jnp.bfloat16), values, preferre...  8.41 us
    dot_general x3, matrix products, score(): jnp.einsum('qhd,khd->hqk', rot_queries, keys, preferred_element_type=jnp....  5.42 us
    unnamed x14, local copies, waits for them, and re-layouts  4.65 us
  transfers between devices with their start and end apart: 3, of which 3 were waited for; matrix products, arithmetic and copies ran while one was open for 13% of the time, Pallas kernels for 0%

commit v1 on v0

v1 whole, which is shorter than its diff:
```python
import math

import jax
import jax.numpy as jnp
import numpy as np
from jax import lax
from jax.experimental import pallas as pl
from jax.experimental.pallas import tpu as pltpu
from jax.sharding import PartitionSpec as P

HEADS = 12
HEAD_DIM = 128
GUIDANCE = 4.0
EPSILON = 1e-06

NX = 4
NC = 2
GROUP_HEADS = HEADS // NX
GW = GROUP_HEADS * HEAD_DIM
SCALE2 = math.log2(math.e) / math.sqrt(HEAD_DIM)
F32 = jnp.float32
BF16 = jnp.bfloat16
MESH = pl.DeviceIdType.MESH


def lane_frequencies():
    time_extent = HEAD_DIM // 8
    space_extent = (HEAD_DIM - time_extent) // 2
    rows = np.zeros((3, HEAD_DIM), np.float32)
    start = 0
    for axis, extent in enumerate((time_extent, space_extent, space_extent)):
        exponent = -np.arange(0, extent, 2).astype(np.float32) / np.float32(extent)
        frequency = (256.0 ** exponent.astype(np.float64)).astype(np.float32)
        rows[axis, start : start + extent] = np.repeat(frequency, 2)
        start += extent
    return rows


def copy_keys(nz):
    half = nz // 2
    keys = [("in", name, d) for name in ("sk", "sv", "q", "fk", "fv") for d in range(1, NX)]
    for kv in ("k", "v"):
        for d in range(NX):
            keys += [("z", kv, 1, d), ("z", kv, nz - 1, d), ("s", kv, 0, d)]
        for r in range(1, nz):
            keys.append(("s", kv, r))
            if r not in (1, nz - 1):
                keys.append(("z", kv, r))
    keys += [("o", d) for d in range(1, NX)]
    keys.append(("cfg",))
    return keys


def kernel(
    nz,
    rows,
    q_hbm,
    fk_hbm,
    fv_hbm,
    sk_hbm,
    sv_hbm,
    tk_hbm,
    tv_hbm,
    shift_hbm,
    scale_hbm,
    proj_hbm,
    cnt_ref,
    pos_ref,
    freq_ref,
    out_ref,
    raw,
    qsend,
    fksend,
    qbuf,
    fkbuf,
    fvbuf,
    kbuf,
    vbuf,
    tkbuf,
    tvbuf,
    shiftbuf,
    scalebuf,
    projbuf,
    qh,
    top,
    total,
    acc,
    osend,
    orecv,
    psend,
    precv,
    local_sem,
    send_sem,
    recv_sem,
):
    keys = {key: i for i, key in enumerate(copy_keys(nz))}
    half = nz // 2
    patch = lax.axis_index("patch")
    branch = lax.axis_index("cfg")
    core = lax.rem(patch, NC)
    x = lax.rem(patch // NC, NX)
    z = patch // (NC * NX)

    def at(zz, xx, cc):
        return {"patch": (zz * NX + xx) * NC + cc}

    def owner(d):
        return lax.rem(x + NX - d, NX)

    def asker(d):
        return lax.rem(x + d, NX)

    up = at(lax.rem(z + 1, nz), x, core)
    down = at(lax.rem(z + nz - 1, nz), x, core)
    sibling = at(z, x, 1 - core)
    partner = {"cfg": 1 - branch}

    started = {}

    def send(key, src, dst, device):
        i = keys[key]
        copy = pltpu.make_async_remote_copy(
            src_ref=src,
            dst_ref=dst,
            send_sem=send_sem.at[i],
            recv_sem=recv_sem.at[i],
            device_id=device,
            device_id_type=MESH,
        )
        copy.start()
        started[key] = copy

    def arrived(key):
        started[key].wait_recv()

    locals_ = {}

    def fetch(name, src, dst):
        copy = pltpu.make_async_copy(src, dst, local_sem.at[len(locals_)])
        copy.start()
        locals_[name] = copy

    def columns(group):
        return pl.ds(pl.multiple_of(group * GW, 128), GW)

    fetch("sk", sk_hbm.at[0, :, columns(x)], kbuf.at[0, 0, 0])
    fetch("sv", sv_hbm.at[0, :, columns(x)], vbuf.at[0, 0, 0])
    fetch("q", q_hbm.at[0], raw.at[0])
    fetch("fk", fk_hbm.at[0], raw.at[1])
    fetch("fv", fv_hbm.at[0, :, columns(x)], fvbuf.at[0])
    fetch("tk", tk_hbm.at[0, :, columns(x)], tkbuf)
    fetch("tv", tv_hbm.at[0, :, columns(x)], tvbuf)
    fetch("shift", shift_hbm, shiftbuf)
    fetch("scale", scale_hbm, scalebuf)
    fetch("proj", proj_hbm, projbuf)

    barrier = pltpu.get_barrier_semaphore()
    friends = [at(z, owner(d), core) for d in range(1, NX)] + [up, down, sibling, partner]
    for friend in friends:
        pl.semaphore_signal(barrier, inc=1, device_id=friend, device_id_type=MESH)
    pl.semaphore_wait(barrier, len(friends))

    for name, hbm, buf in (("sk", sk_hbm, kbuf), ("sv", sv_hbm, vbuf)):
        for d in range(1, NX):
            send(
                ("in", name, d),
                hbm.at[0, :, columns(owner(d))],
                buf.at[0, 0, d],
                at(z, owner(d), core),
            )

    def spread(kv, buf, d):
        send(("z", kv, 1, d), buf.at[0, 0, d], buf.at[1, 0, d], up)
        send(("z", kv, nz - 1, d), buf.at[0, 0, d], buf.at[nz - 1, 0, d], down)
        send(("s", kv, 0, d), buf.at[0, 0, d], buf.at[0, 1, d], sibling)

    locals_["sk"].wait()
    spread("k", kbuf, 0)
    locals_["sv"].wait()
    spread("v", vbuf, 0)

    at_row = lax.broadcasted_iota(jnp.int32, (rows, rows), 0)
    at_col = lax.broadcasted_iota(jnp.int32, (rows, rows), 1)
    places = pos_ref[...].astype(F32)
    angles = jnp.zeros((rows, HEAD_DIM), F32)
    for axis in range(3):
        column = jnp.sum(
            jnp.where(at_row == at_col, places[axis : axis + 1, :], 0.0), axis=1, keepdims=True
        )
        angles = angles + column * freq_ref[axis : axis + 1, :]
    even = lax.rem(lax.broadcasted_iota(jnp.int32, (rows, HEAD_DIM), 1), 2) == 0
    cosine = jnp.cos(angles)
    sine = jnp.sin(angles)
    sine = jnp.where(even, -sine, sine)
    locals_["q"].wait()
    locals_["fk"].wait()
    for which, name, sendbuf, ownbuf in ((0, "q", qsend, qbuf), (1, "fk", fksend, fkbuf)):
        for d in range(NX):
            for h in range(GROUP_HEADS):
                lanes = pl.ds(pl.multiple_of(owner(d) * GW + h * HEAD_DIM, 128), HEAD_DIM)
                value = raw[which, :, lanes].astype(F32)
                other = jnp.where(
                    even,
                    pltpu.roll(value, HEAD_DIM - 1, 1),
                    pltpu.roll(value, 1, 1),
                )
                turned = (value * cosine + other * sine).astype(BF16)
                target = ownbuf if d == 0 else sendbuf
                target[max(d - 1, 0) if d else 0, :, h * HEAD_DIM : (h + 1) * HEAD_DIM] = turned
            if d:
                send(("in", name, d), sendbuf.at[d - 1], ownbuf.at[d], at(z, owner(d), core))
    for d in range(1, NX):
        send(
            ("in", "fv", d),
            fv_hbm.at[0, :, columns(owner(d))],
            fvbuf.at[d],
            at(z, owner(d), core),
        )

    for name, kv, buf in (("sk", "k", kbuf), ("sv", "v", vbuf)):
        for d in range(1, NX):
            arrived(("in", name, d))
            spread(kv, buf, d)

    def lanes_of(h):
        return slice(h * HEAD_DIM, (h + 1) * HEAD_DIM)

    def stacked(buf, h, slots):
        pieces = [
            buf[slot + (d,)][:, lanes_of(h)].astype(F32) for slot in slots for d in range(NX)
        ]
        return jnp.concatenate(pieces, axis=0).astype(BF16)

    def scores_of(h, tile):
        return lax.dot_general(
            qh[h], tile, (((1,), (1,)), ((), ())), preferred_element_type=F32
        )

    def weigh(weights, tile):
        return jnp.dot(weights.astype(BF16), tile, preferred_element_type=F32)

    all_rows = NX * rows
    for d in range(1, NX):
        arrived(("in", "q", d))
    for h in range(GROUP_HEADS):
        qh[h] = stacked(qbuf, h, [()])
    for d in range(1, NX):
        arrived(("in", "fk", d))
        arrived(("in", "fv", d))
    locals_["fv"].wait()
    locals_["tk"].wait()
    locals_["tv"].wait()
    block_row = lax.broadcasted_iota(jnp.int32, (all_rows, all_rows), 0) // rows
    block_col = lax.broadcasted_iota(jnp.int32, (all_rows, all_rows), 1) // rows
    same = block_row == block_col
    words = tkbuf.shape[0]
    live = lax.broadcasted_iota(jnp.int32, (all_rows, words), 1) < cnt_ref[0]
    for h in range(GROUP_HEADS):
        own = jnp.where(
            same,
            scores_of(h, stacked(fkbuf, h, [()])),
            scores_of(h, stacked(kbuf, h, [(0, 0)])),
        )
        word = jnp.where(live, scores_of(h, tkbuf[:, lanes_of(h)]), -jnp.inf)
        high = jnp.maximum(
            jnp.max(own, axis=1, keepdims=True), jnp.max(word, axis=1, keepdims=True)
        )
        own = jnp.exp2((own - high) * SCALE2)
        word = jnp.exp2((word - high) * SCALE2)
        top[h] = high
        total[h] = jnp.sum(own, axis=1, keepdims=True) + jnp.sum(word, axis=1, keepdims=True)
        acc[h] = (
            weigh(jnp.where(same, own, 0.0), stacked(fvbuf, h, [()]))
            + weigh(jnp.where(same, 0.0, own), stacked(vbuf, h, [(0, 0)]))
            + weigh(word, tvbuf[:, lanes_of(h)])
        )

    def absorb(slots):
        for h in range(GROUP_HEADS):
            score = scores_of(h, stacked(kbuf, h, slots))
            old = top[h]
            high = jnp.maximum(old, jnp.max(score, axis=1, keepdims=True))
            weights = jnp.exp2((score - high) * SCALE2)
            rescale = jnp.exp2((old - high) * SCALE2)
            top[h] = high
            total[h] = total[h] * rescale + jnp.sum(weights, axis=1, keepdims=True)
            acc[h] = acc[h] * rescale + weigh(weights, stacked(vbuf, h, slots))

    def sibling_arrived(r):
        for kv in ("k", "v"):
            if r == 0:
                for d in range(NX):
                    arrived(("s", kv, 0, d))
            else:
                arrived(("s", kv, r))

    pending = [0]
    for t in range(1, half + 1):
        here = []
        for kv, buf in (("k", kbuf), ("v", vbuf)):
            for r, step, device in ((t, 1, up), (nz - t, -1, down)):
                if t == half and (kv == "k") != (step == 1):
                    continue
                if t == 1:
                    for d in range(NX):
                        arrived(("z", kv, r, d))
                else:
                    arrived(("z", kv, r))
                following = r + step
                last = following == half
                crossed = (r < half) == (step == 1) and r != half
                if crossed and (not last or (kv == "k") == (step == 1)):
                    send(("z", kv, following), buf.at[r, 0], buf.at[following, 0], device)
                send(("s", kv, r), buf.at[r, 0], buf.at[r, 1], sibling)
                if r not in here:
                    here.append(r)
        for r in pending:
            sibling_arrived(r)
        absorb([(r, 0) for r in here] + [(r, 1) for r in pending])
        pending = here
    for r in pending:
        sibling_arrived(r)
    absorb([(r, 1) for r in pending])

    for h in range(GROUP_HEADS):
        attended = acc[h] / total[h]
        for d in range(NX):
            osend[d, :, lanes_of(h)] = attended[d * rows : (d + 1) * rows, :]
    for d in range(1, NX):
        send(("o", d), osend.at[d], orecv.at[x], at(z, asker(d), core))
    orecv[x] = osend[0]
    for name in ("shift", "scale", "proj"):
        locals_[name].wait()
    for d in range(1, NX):
        arrived(("o", d))

    features = HEADS * HEAD_DIM
    parts = [orecv[g] for g in range(NX)]
    mean = sum(jnp.sum(part, axis=1, keepdims=True) for part in parts) / features
    parts = [part - mean for part in parts]
    spread_ = sum(jnp.sum(part * part, axis=1, keepdims=True) for part in parts) / features
    inverse = lax.rsqrt(spread_ + EPSILON)
    predicted = None
    for g in range(NX):
        wide = slice(g * GW, (g + 1) * GW)
        modulated = parts[g] * inverse * (1.0 + scalebuf[:, wide]) + shiftbuf[:, wide]
        term = jnp.dot(modulated.astype(BF16), projbuf[wide, :], preferred_element_type=F32)
        predicted = term if predicted is None else predicted + term
    width = predicted.shape[1] // 2
    low, high_half = predicted[:, :width], predicted[:, width:]
    first = branch == 0
    psend[...] = jnp.where(first, high_half, low)
    send(("cfg",), psend, precv, partner)
    keep = jnp.where(first, low, high_half)
    own_weight = jnp.where(first, 1.0 - GUIDANCE, GUIDANCE)
    other_weight = jnp.where(first, GUIDANCE, 1.0 - GUIDANCE)
    arrived(("cfg",))
    out_ref[0] = own_weight * keep + other_weight * precv[...]
    for copy in started.values():
        copy.wait_send()


def shards(nz, *args):
    (q, fk, fv, sk, sv, tk, tv, count, positions, shift, scale, proj) = args
    rows, features = q.shape[1], q.shape[2]
    words = tk.shape[1]
    width = proj.shape[1] // 2
    n_copies = len(copy_keys(nz))
    anywhere = pl.BlockSpec(memory_space=pl.ANY)
    in_vmem = pl.BlockSpec(memory_space=pltpu.VMEM)

    def body(*refs):
        kernel(nz, rows, *refs)

    return pl.pallas_call(
        body,
        out_shape=jax.ShapeDtypeStruct((1, rows, width), F32),
        in_specs=[anywhere] * 10
        + [pl.BlockSpec(memory_space=pltpu.SMEM), in_vmem, in_vmem],
        out_specs=in_vmem,
        scratch_shapes=[
            pltpu.VMEM((2, rows, features), BF16),
            pltpu.VMEM((NX - 1, rows, GW), BF16),
            pltpu.VMEM((NX - 1, rows, GW), BF16),
            pltpu.VMEM((NX, rows, GW), BF16),
            pltpu.VMEM((NX, rows, GW), BF16),
            pltpu.VMEM((NX, rows, GW), BF16),
            pltpu.VMEM((nz, NC, NX, rows, GW), BF16),
            pltpu.VMEM((nz, NC, NX, rows, GW), BF16),
            pltpu.VMEM((words, GW), BF16),
            pltpu.VMEM((words, GW), BF16),
            pltpu.VMEM((1, features), F32),
            pltpu.VMEM((1, features), F32),
            pltpu.VMEM((features, 2 * width), BF16),
            pltpu.VMEM((GROUP_HEADS, NX * rows, HEAD_DIM), BF16),
            pltpu.VMEM((GROUP_HEADS, NX * rows, 1), F32),
            pltpu.VMEM((GROUP_HEADS, NX * rows, 1), F32),
            pltpu.VMEM((GROUP_HEADS, NX * rows, HEAD_DIM), F32),
            pltpu.VMEM((NX, rows, GW), F32),
            pltpu.VMEM((NX, rows, GW), F32),
            pltpu.VMEM((rows, width), F32),
            pltpu.VMEM((rows, width), F32),
            pltpu.SemaphoreType.DMA((10,)),
            pltpu.SemaphoreType.DMA((n_copies,)),
            pltpu.SemaphoreType.DMA((n_copies,)),
        ],
        compiler_params=pltpu.CompilerParams(
            collective_id=0, has_side_effects=True, vmem_limit_bytes=48 * 1024 * 1024
        ),
        name="stale_attention",
    )(q, fk, fv, sk, sv, tk, tv, shift, scale, proj, count, positions, jnp.asarray(lane_frequencies()))


def solution(mesh):
    nz = mesh.shape["patch"] // (NX * NC)
    placed = (
        P("cfg", "patch", "rep"),
        P("cfg", "patch", "rep"),
        P("cfg", "patch", "rep"),
        P("cfg", "patch", "rep"),
        P("cfg", "patch", "rep"),
        P("cfg", "rep", None),
        P("cfg", "rep", None),
        P("cfg"),
        P("rep", "patch"),
        P("cfg", None),
        P("cfg", None),
        P(),
    )

    def run(*args):
        return shards(nz, *args)

    return jax.shard_map(
        run, mesh=mesh, in_specs=placed, out_specs=P("cfg", "patch", "rep"), check_vma=False
    )
```

time: 225 us -> 57.2 us (0.25)
  waiting for transfers between devices: 157 us -> 0 us
  Pallas kernels: 0 us -> 50.6 us
  local copies, waits for them, and re-layouts: 30 us -> 5.14 us
  matrix products: 14.1 us -> 0 us
  between operations: 14.3 us -> 0.81 us
  other arithmetic: 6.08 us -> 0 us
  starting transfers between devices: 3.18 us -> 0 us
    all_gather x2 -> x0, waiting for transfers between devices: 154 us -> none  [the longest x1 84.2 us: shards(): lax.all_gather(stale_keys, 'patch', axis=1, tiled=True)]
    pallas_call x0 -> x1, Pallas kernels: none -> 50.6 us  [shards(): pl.pallas_call(body, out_shape=jax.ShapeDtypeStruct((1, rows, width), F32...]
    all_gather x2 -> x0, local copies, waits for them, and re-layouts: 20.8 us -> none  [the longest x1 10.4 us: shards(): lax.all_gather(stale_values, 'patch', axis=1, tiled=True)]
    dot_general x7 -> x0, matrix products: 14.1 us -> none  [the longest x3 8.41 us: absorb(): jnp.einsum('hqk,khd->hqd', weights.astype(jnp.bfloat16), values, preferre...]
    another operation x3 -> x0, other arithmetic: 4.25 us -> none
    ppermute x1 -> x0, starting transfers between devices: 3.11 us -> none  [partner_2(): lax.ppermute(shard, axis, [(i, i ^ 1 << stride) for i in range(lax.axis_s...]
    unnamed x14 -> x23, local copies, waits for them, and re-layouts: 4.65 us -> 4.46 us
  transfers between devices with their start and end apart: 3 -> 0, of which waited for: 3 -> 0; matrix products, arithmetic and copies ran while one was open for 13% -> 0% of each run, Pallas kernels for 0% -> 0%
where the time goes in v1:
time: 57.2 us; the launch traced here: 56.5 us
  Pallas kernels  50.6 us (88%)
  local copies, waits for them, and re-layouts  5.14 us (9%)
  between operations  0.81 us (1%)
    pallas_call x1, Pallas kernels, shards(): pl.pallas_call(body, out_shape=jax.ShapeDtypeStruct((1, rows, width), F32...  50.6 us
    unnamed x23, local copies, waits for them, and re-layouts  4.46 us

profile of v1, /device:TPU:1, one launch (start us, length us, event | category | flops | bytes accessed | tf_op | source)
XLA Modules:
  0.0 56.5 jit_solution(10343149297702620290)
XLA Ops:
  0.7 0.0 copy-start.2
  0.7 0.0 copy-start.3
  0.7 0.0 copy-start.4
  0.7 0.0 copy-start.5
  0.7 0.0 copy-start.7
  0.7 0.0 copy-start.8
  0.7 0.0 copy-start.9
  0.7 0.0 copy-start.10
  0.7 1.3 %copy.14.refs_9_ = bf16[1536,64]{1,0:T(8,128)(2,1)S(1)} copy(bf16[1536,64]{0,1:T(8,128)(2,1)} %param.24) | data formatting | bytes 393216 | tf_op args[11]
  2.0 0.0 copy-done.2
  2.0 0.0 copy-done.3
  2.0 0.0 copy-done.4
  2.0 0.0 copy-done.5
  2.0 0.0 copy-done.7
  2.1 0.0 copy-done.8
  2.1 0.0 copy-done.9
  2.1 0.0 copy-done.10
  2.1 0.0 copy-start
  2.1 1.1 %copy-done = bf16[1,256,1536]{2,1,0:T(8,128)(2,1)S(1)} copy-done((bf16[1,256,1536]{2,1,0:T(8,128)(2,1)S(1)}, bf16[1,256,1536]{2,1,0:T(8,128)(2,1)}, u32[]{:S(2)}) %copy-start) | copy-done | bytes 786456
  3.2 0.0 copy-start.1
  3.2 1.1 %copy-done.1 = bf16[1,256,1536]{2,1,0:T(8,128)(2,1)S(1)} copy-done((bf16[1,256,1536]{2,1,0:T(8,128)(2,1)S(1)}, bf16[1,256,1536]{2,1,0:T(8,128)(2,1)}, u32[]{:S(2)}) %copy-start.1) | copy-done | bytes 786456
  4.4 0.9 %copy-done.6 = bf16[1,40,1536]{2,1,0:T(8,128)(2,1)S(1)} copy-done((bf16[1,40,1536]{2,1,0:T(8,128)(2,1)S(1)}, bf16[1,40,1536]{2,1,0:T(8,128)(2,1)}, u32[]{:S(2)}) %copy-start.6) | copy-done | bytes 122904
  5.3 50.6 %stale_attention.1 = f32[1,40,32]{2,1,0:T(8,128)S(1)} custom-call(bf16[1,40,1536]{2,1,0:T(8,128)(2,1)S(1)} %copy-done.2, bf16[1,40,1536]{2,1,0:T(8,128)(2,1)S(1)} %copy-done.3, bf16[1,40,1536]{2,1,0:T(8,128)(2,1)S(1)} %copy-done.4, bf16[1,40,1536]{2,1,0:T(8,128)(2,1)S(1)} %copy-done.5, bf16[1,40,1536]{2,1,0:T(8,128)(2,1)S(1)} %copy-done.6, ...), custom_call_target="tpu_custom_call" | custom-call | tf_op jit(solution)/shard_map/stale_attention/pallas_call | solution.py:375
  55.8 0.7 %copy.15 = f32[1,40,32]{1,2,0:T(8,128)} copy(f32[1,40,32]{2,1,0:T(8,128)S(1)} %stale_attention.1) | data formatting | bytes 10240 | tf_op jit(solution)/shard_map/stale_attention/pallas_call | solution.py:375
  (1 shorter events, 0.0 us)
Async XLA Ops:
  0.7 1.4 %copy-start.2 = (bf16[1,40,1536]{2,1,0:T(8,128)(2,1)S(1)}, bf16[1,40,1536]{2,1,0:T(8,128)(2,1)}, u32[]{:S(2)}) copy-start(bf16[1,40,1536]{2,1,0:T(8,128)(2,1)} %refs_0_.1) | copy-start | bytes 368644
  0.7 1.4 %copy-start.3 = (bf16[1,40,1536]{2,1,0:T(8,128)(2,1)S(1)}, bf16[1,40,1536]{2,1,0:T(8,128)(2,1)}, u32[]{:S(2)}) copy-start(bf16[1,40,1536]{2,1,0:T(8,128)(2,1)} %refs_1_.1) | copy-start | bytes 368644
  0.7 1.4 %copy-start.4 = (bf16[1,40,1536]{2,1,0:T(8,128)(2,1)S(1)}, bf16[1,40,1536]{2,1,0:T(8,128)(2,1)}, u32[]{:S(2)}) copy-start(bf16[1,40,1536]{2,1,0:T(8,128)(2,1)} %refs_2_.1) | copy-start | bytes 368644
  0.7 1.4 %copy-start.5 = (bf16[1,40,1536]{2,1,0:T(8,128)(2,1)S(1)}, bf16[1,40,1536]{2,1,0:T(8,128)(2,1)}, u32[]{:S(2)}) copy-start(bf16[1,40,1536]{2,1,0:T(8,128)(2,1)} %refs_3_.1) | copy-start | bytes 368644
  0.7 1.4 %copy-start.7 = (f32[1,1536]{1,0:T(1,128)S(1)}, f32[1,1536]{1,0:T(1,128)}, u32[]{:S(2)}) copy-start(f32[1,1536]{1,0:T(1,128)} %refs_7_.1) | copy-start | bytes 18436
  0.7 1.4 %copy-start.8 = (f32[1,1536]{1,0:T(1,128)S(1)}, f32[1,1536]{1,0:T(1,128)}, u32[]{:S(2)}) copy-start(f32[1,1536]{1,0:T(1,128)} %refs_8_.1) | copy-start | bytes 18436
  0.7 1.4 %copy-start.9 = (s32[3,40]{1,0:T(4,128)S(1)}, s32[3,40]{1,0:T(4,128)}, u32[]{:S(2)}) copy-start(s32[3,40]{1,0:T(4,128)} %refs_11_.1) | copy-start | bytes 1444
  0.7 1.4 %copy-start.10 = (f32[3,128]{1,0:T(4,128)S(1)}, f32[3,128]{1,0:T(4,128)}, u32[]{:S(2)}) copy-start(f32[3,128]{1,0:T(4,128)} %constant.2.clone.refs_12_) | copy-start | bytes 4612
  2.1 1.1 %copy-start = (bf16[1,256,1536]{2,1,0:T(8,128)(2,1)S(1)}, bf16[1,256,1536]{2,1,0:T(8,128)(2,1)}, u32[]{:S(2)}) copy-start(bf16[1,256,1536]{2,1,0:T(8,128)(2,1)} %refs_5_.1) | copy-start | bytes 2359300
  3.2 1.1 %copy-start.1 = (bf16[1,256,1536]{2,1,0:T(8,128)(2,1)S(1)}, bf16[1,256,1536]{2,1,0:T(8,128)(2,1)}, u32[]{:S(2)}) copy-start(bf16[1,256,1536]{2,1,0:T(8,128)(2,1)} %refs_6_.1) | copy-start | bytes 2359300
  4.4 0.9 %copy-start.6 = (bf16[1,40,1536]{2,1,0:T(8,128)(2,1)S(1)}, bf16[1,40,1536]{2,1,0:T(8,128)(2,1)}, u32[]{:S(2)}) copy-start(bf16[1,40,1536]{2,1,0:T(8,128)(2,1)} %refs_4_.1) | copy-start | bytes 368644

commit v2 on v1

v2 whole, which is shorter than its diff:
```python
import math

import jax
import jax.numpy as jnp
import numpy as np
from jax import lax
from jax.experimental import pallas as pl
from jax.experimental.pallas import tpu as pltpu
from jax.sharding import PartitionSpec as P

HEADS = 12
HEAD_DIM = 128
GUIDANCE = 4.0
EPSILON = 1e-06

NX = 4
NC = 2
NEAREST = (1, 3, 2)
GROUP_HEADS = HEADS // NX
GW = GROUP_HEADS * HEAD_DIM
SCALE2 = math.log2(math.e) / math.sqrt(HEAD_DIM)
SIDE = 64
F32 = jnp.float32
BF16 = jnp.bfloat16
MESH = pl.DeviceIdType.MESH


def lane_frequencies():
    time_extent = HEAD_DIM // 8
    space_extent = (HEAD_DIM - time_extent) // 2
    rows = np.zeros((3, HEAD_DIM), np.float32)
    start = 0
    for axis, extent in enumerate((time_extent, space_extent, space_extent)):
        exponent = -np.arange(0, extent, 2).astype(np.float32) / np.float32(extent)
        frequency = (256.0 ** exponent.astype(np.float64)).astype(np.float32)
        rows[axis, start : start + extent] = np.repeat(frequency, 2)
        start += extent
    return rows


def copy_keys(nz):
    keys = [("in", name, d) for name in ("sk", "sv", "q", "fk", "fv") for d in range(1, NX)]
    for kv in ("k", "v"):
        for d in range(NX):
            keys += [("z", kv, 1, d), ("z", kv, nz - 1, d)]
        keys.append(("s", kv, 0))
        for r in range(1, nz):
            keys.append(("s", kv, r))
            if r not in (1, nz - 1):
                keys.append(("z", kv, r))
    keys += [("own", d) for d in range(1, NX)]
    keys += [("other", d) for d in range(NX)]
    return keys


def kernel(
    nz,
    rows,
    q_hbm,
    fk_hbm,
    fv_hbm,
    sk_hbm,
    sv_hbm,
    tk_hbm,
    tv_hbm,
    shift_hbm,
    scale_hbm,
    proj_hbm,
    pos_hbm,
    freq_hbm,
    cnt_ref,
    out_ref,
    raw,
    qsend,
    fksend,
    qbuf,
    fkbuf,
    fvbuf,
    kbuf,
    vbuf,
    tkbuf,
    tvbuf,
    shiftbuf,
    scalebuf,
    projbuf,
    pos_ref,
    freq_ref,
    qh,
    top,
    total,
    acc,
    ysend,
    yrecv,
    local_sem,
    send_sem,
    recv_sem,
):
    keys = {key: i for i, key in enumerate(copy_keys(nz))}
    half = nz // 2
    patch = lax.axis_index("patch")
    branch = lax.axis_index("cfg")
    core = lax.rem(patch, NC)
    x = lax.rem(patch // NC, NX)
    z = patch // (NC * NX)

    def at(zz, xx, cc):
        return {"patch": (zz * NX + xx) * NC + cc}

    def owner(d):
        return lax.rem(x + NX - d, NX)

    def asker(d):
        return lax.rem(x + d, NX)

    up = at(lax.rem(z + 1, nz), x, core)
    down = at(lax.rem(z + nz - 1, nz), x, core)
    sibling = at(z, x, 1 - core)

    def across(xx):
        return {"cfg": 1 - branch, **at(z, xx, core)}

    started = {}

    def send(key, src, dst, device):
        i = keys[key]
        copy = pltpu.make_async_remote_copy(
            src_ref=src,
            dst_ref=dst,
            send_sem=send_sem.at[i],
            recv_sem=recv_sem.at[i],
            device_id=device,
            device_id_type=MESH,
        )
        copy.start()
        started[key] = copy

    def arrived(key):
        started[key].wait_recv()

    locals_ = {}

    def fetch(name, src, dst):
        copy = pltpu.make_async_copy(src, dst, local_sem.at[len(locals_)])
        copy.start()
        locals_[name] = copy

    def columns(group):
        return pl.ds(pl.multiple_of(group * GW, 128), GW)

    fetch("pos", pos_hbm, pos_ref)
    fetch("freq", freq_hbm, freq_ref)
    fetch("sk", sk_hbm.at[0, :, columns(x)], kbuf.at[0, 0, 0])
    fetch("sv", sv_hbm.at[0, :, columns(x)], vbuf.at[0, 0, 0])
    fetch("q", q_hbm.at[0], raw.at[0])
    fetch("fk", fk_hbm.at[0], raw.at[1])
    fetch("fv", fv_hbm.at[0, :, columns(x)], fvbuf.at[0])
    fetch("tk", tk_hbm.at[0, :, columns(x)], tkbuf)
    fetch("tv", tv_hbm.at[0, :, columns(x)], tvbuf)
    fetch("shift", shift_hbm.at[:, columns(x)], shiftbuf)
    fetch("scale", scale_hbm.at[:, columns(x)], scalebuf)
    fetch("proj", proj_hbm.at[:, columns(x)], projbuf)

    barrier = pltpu.get_barrier_semaphore()
    friends = [at(z, owner(d), core) for d in range(1, NX)] + [up, down, sibling]
    friends += [across(owner(d)) for d in range(NX)]
    for friend in friends:
        pl.semaphore_signal(barrier, inc=1, device_id=friend, device_id_type=MESH)
    pl.semaphore_wait(barrier, len(friends))

    for name, hbm, buf in (("sk", sk_hbm, kbuf), ("sv", sv_hbm, vbuf)):
        for d in NEAREST:
            send(
                ("in", name, d),
                hbm.at[0, :, columns(owner(d))],
                buf.at[0, 0, d],
                at(z, owner(d), core),
            )

    def spread(kv, buf, d):
        send(("z", kv, 1, d), buf.at[0, 0, d], buf.at[1, 0, d], up)
        send(("z", kv, nz - 1, d), buf.at[0, 0, d], buf.at[nz - 1, 0, d], down)

    locals_["sk"].wait()
    spread("k", kbuf, 0)
    locals_["sv"].wait()
    spread("v", vbuf, 0)

    at_row = lax.broadcasted_iota(jnp.int32, (rows, rows), 0)
    at_col = lax.broadcasted_iota(jnp.int32, (rows, rows), 1)
    locals_["pos"].wait()
    locals_["freq"].wait()
    places = pos_ref[...].astype(F32)
    angles = jnp.zeros((rows, HEAD_DIM), F32)
    for axis in range(3):
        column = jnp.sum(
            jnp.where(at_row == at_col, places[axis : axis + 1, :], 0.0), axis=1, keepdims=True
        )
        angles = angles + column * freq_ref[axis : axis + 1, :]
    even = lax.rem(lax.broadcasted_iota(jnp.int32, (rows, HEAD_DIM), 1), 2) == 0
    cosine = jnp.cos(angles)
    sine = jnp.sin(angles)
    sine = jnp.where(even, -sine, sine)
    locals_["q"].wait()
    locals_["fk"].wait()
    for which, name, sendbuf, ownbuf in ((0, "q", qsend, qbuf), (1, "fk", fksend, fkbuf)):
        for d in range(NX):
            for h in range(GROUP_HEADS):
                lanes = pl.ds(pl.multiple_of(owner(d) * GW + h * HEAD_DIM, 128), HEAD_DIM)
                value = raw[which, :, lanes].astype(F32)
                other = jnp.where(
                    even,
                    pltpu.roll(value, HEAD_DIM - 1, 1),
                    pltpu.roll(value, 1, 1),
                )
                turned = (value * cosine + other * sine).astype(BF16)
                target = ownbuf if d == 0 else sendbuf
                target[max(d - 1, 0) if d else 0, :, h * HEAD_DIM : (h + 1) * HEAD_DIM] = turned

    for name, kv, buf in (("sk", "k", kbuf), ("sv", "v", vbuf)):
        for d in NEAREST:
            arrived(("in", name, d))
            spread(kv, buf, d)
    for kv, buf in (("k", kbuf), ("v", vbuf)):
        send(("s", kv, 0), buf.at[0, 0], buf.at[0, 1], sibling)
    for d in NEAREST:
        send(("in", "q", d), qsend.at[d - 1], qbuf.at[d], at(z, owner(d), core))
    for d in NEAREST:
        send(("in", "fk", d), fksend.at[d - 1], fkbuf.at[d], at(z, owner(d), core))
        send(
            ("in", "fv", d),
            fv_hbm.at[0, :, columns(owner(d))],
            fvbuf.at[d],
            at(z, owner(d), core),
        )

    def lanes_of(h):
        return slice(h * HEAD_DIM, (h + 1) * HEAD_DIM)

    def stacked(buf, h, slots):
        pieces = [
            buf[slot + (d,)][:, lanes_of(h)].astype(F32) for slot in slots for d in range(NX)
        ]
        return jnp.concatenate(pieces, axis=0).astype(BF16)

    def scores_of(h, tile):
        return lax.dot_general(
            qh[h], tile, (((1,), (1,)), ((), ())), preferred_element_type=F32
        )

    def weigh(weights, tile):
        return jnp.dot(weights.astype(BF16), tile, preferred_element_type=F32)

    all_rows = NX * rows

    def begin():
        for d in range(1, NX):
            arrived(("in", "q", d))
        for h in range(GROUP_HEADS):
            qh[h] = stacked(qbuf, h, [()])
        for d in range(1, NX):
            arrived(("in", "fk", d))
            arrived(("in", "fv", d))
        locals_["fv"].wait()
        locals_["tk"].wait()
        locals_["tv"].wait()
        block_row = lax.broadcasted_iota(jnp.int32, (all_rows, all_rows), 0) // rows
        block_col = lax.broadcasted_iota(jnp.int32, (all_rows, all_rows), 1) // rows
        same = block_row == block_col
        words = tkbuf.shape[0]
        live = lax.broadcasted_iota(jnp.int32, (all_rows, words), 1) < cnt_ref[0]
        for h in range(GROUP_HEADS):
            own = jnp.where(
                same,
                scores_of(h, stacked(fkbuf, h, [()])),
                scores_of(h, stacked(kbuf, h, [(0, 0)])),
            )
            word = jnp.where(live, scores_of(h, tkbuf[:, lanes_of(h)]), -jnp.inf)
            high = jnp.maximum(
                jnp.max(own, axis=1, keepdims=True), jnp.max(word, axis=1, keepdims=True)
            )
            own = jnp.exp2((own - high) * SCALE2)
            word = jnp.exp2((word - high) * SCALE2)
            top[h] = high
            total[h] = jnp.sum(own, axis=1, keepdims=True) + jnp.sum(word, axis=1, keepdims=True)
            acc[h] = (
                weigh(jnp.where(same, own, 0.0), stacked(fvbuf, h, [()]))
                + weigh(jnp.where(same, 0.0, own), stacked(vbuf, h, [(0, 0)]))
                + weigh(word, tvbuf[:, lanes_of(h)])
            )


    def absorb(slots):
        for h in range(GROUP_HEADS):
            score = scores_of(h, stacked(kbuf, h, slots))
            old = top[h]
            high = jnp.maximum(old, jnp.max(score, axis=1, keepdims=True))
            weights = jnp.exp2((score - high) * SCALE2)
            rescale = jnp.exp2((old - high) * SCALE2)
            top[h] = high
            total[h] = total[h] * rescale + jnp.sum(weights, axis=1, keepdims=True)
            acc[h] = acc[h] * rescale + weigh(weights, stacked(vbuf, h, slots))

    def sibling_arrived(r):
        for kv in ("k", "v"):
            arrived(("s", kv, r))

    pending = [0]
    for t in range(1, half + 1):
        if t == half:
            for r in pending:
                sibling_arrived(r)
            absorb([(r, 1) for r in pending])
            pending = []
        here = []
        for kv, buf in (("k", kbuf), ("v", vbuf)):
            for r, step, device in ((t, 1, up), (nz - t, -1, down)):
                if t == half and (kv == "k") != (step == 1):
                    continue
                if t == 1:
                    for d in range(NX):
                        arrived(("z", kv, r, d))
                else:
                    arrived(("z", kv, r))
                following = r + step
                if t < half and (following != half or (kv == "k") == (step == 1)):
                    send(("z", kv, following), buf.at[r, 0], buf.at[following, 0], device)
                if r not in here:
                    here.append(r)
            for r in here:
                send(("s", kv, r), buf.at[r, 0], buf.at[r, 1], sibling)
        if t == 1:
            begin()
        for r in pending:
            sibling_arrived(r)
        absorb([(r, 0) for r in here] + [(r, 1) for r in pending])
        pending = here
    for r in pending:
        sibling_arrived(r)
    absorb([(r, 1) for r in pending])

    for name in ("shift", "scale", "proj"):
        locals_[name].wait()
    width = projbuf.shape[0] // 2
    gap = jnp.zeros((SIDE - width, GW), BF16)
    channels = jnp.concatenate([projbuf[:width], gap, projbuf[width:], gap], axis=0)

    def project(value, h):
        tile = channels[:, lanes_of(h)]
        big = value.astype(BF16)
        small = (value - big.astype(F32)).astype(BF16)
        nt = (((1,), (1,)), ((), ()))
        return lax.dot_general(
            big, tile, nt, preferred_element_type=F32
        ) + lax.dot_general(small, tile, nt, preferred_element_type=F32)

    gain = 1.0 + scalebuf[...]
    affine = jnp.concatenate([gain, shiftbuf[...], jnp.zeros((6, GW), F32)], axis=0)
    affine = sum(project(affine[:, lanes_of(h)], h) for h in range(GROUP_HEADS))
    attended = [acc[h] / total[h] for h in range(GROUP_HEADS)]
    mean = sum(jnp.sum(part, axis=1, keepdims=True) for part in attended) / GW
    attended = [part - mean for part in attended]
    squares = sum(jnp.sum(part * part, axis=1, keepdims=True) for part in attended)
    share = sum(project(attended[h] * gain[:, lanes_of(h)], h) for h in range(GROUP_HEADS))
    lane = lax.rem(lax.broadcasted_iota(jnp.int32, share.shape, 1), SIDE)
    share = jnp.where(lane == width, mean, jnp.where(lane == width + 1, squares, share))
    for d in range(NX):
        ysend[d, :rows] = share[d * rows : (d + 1) * rows]
        ysend[d, rows:] = affine
    for d in NEAREST:
        send(("own", d), ysend.at[d], yrecv.at[0, d], at(z, asker(d), core))
    for d in (0,) + NEAREST:
        send(("other", d), ysend.at[d], yrecv.at[1, d], across(asker(d)))
    yrecv[0, 0] = ysend[0]
    for d in NEAREST:
        arrived(("own", d))
    for d in range(NX):
        arrived(("other", d))

    def prediction(side):
        blocks = [yrecv[side, d] for d in range(NX)]
        means = [block[:rows, width : width + 1] for block in blocks]
        middle = sum(means) / NX
        spread_ = sum(block[:rows, width + 1 : width + 2] for block in blocks)
        spread_ = spread_ + GW * sum((mean_ - middle) * (mean_ - middle) for mean_ in means)
        inverse = lax.rsqrt(spread_ / (NX * GW) + EPSILON)
        linear = sum(
            block[:rows] + (mean_ - middle) * block[rows : rows + 1]
            for block, mean_ in zip(blocks, means)
        )
        return inverse * linear + sum(block[rows + 1 : rows + 2] for block in blocks)

    first = branch == 0
    own_weight = jnp.where(first, 1.0 - GUIDANCE, GUIDANCE)
    other_weight = jnp.where(first, GUIDANCE, 1.0 - GUIDANCE)
    guided = (own_weight * prediction(0) + other_weight * prediction(1)).T
    out_ref[0] = jnp.where(first, guided[:width], guided[SIDE : SIDE + width])
    for copy in started.values():
        copy.wait_send()


def shards(nz, *args):
    (q, fk, fv, sk, sv, tk, tv, count, positions, shift, scale, proj) = args
    rows, features = q.shape[1], q.shape[2]
    words = tk.shape[1]
    width = proj.shape[1] // 2
    n_copies = len(copy_keys(nz))
    anywhere = pl.BlockSpec(memory_space=pl.ANY)
    in_vmem = pl.BlockSpec(memory_space=pltpu.VMEM)

    def body(*refs):
        kernel(nz, rows, *refs)

    guided = pl.pallas_call(
        body,
        out_shape=jax.ShapeDtypeStruct((1, width, rows), F32),
        in_specs=[anywhere] * 12 + [pl.BlockSpec(memory_space=pltpu.SMEM)],
        out_specs=in_vmem,
        scratch_shapes=[
            pltpu.VMEM((2, rows, features), BF16),
            pltpu.VMEM((NX - 1, rows, GW), BF16),
            pltpu.VMEM((NX - 1, rows, GW), BF16),
            pltpu.VMEM((NX, rows, GW), BF16),
            pltpu.VMEM((NX, rows, GW), BF16),
            pltpu.VMEM((NX, rows, GW), BF16),
            pltpu.VMEM((nz, NC, NX, rows, GW), BF16),
            pltpu.VMEM((nz, NC, NX, rows, GW), BF16),
            pltpu.VMEM((words, GW), BF16),
            pltpu.VMEM((words, GW), BF16),
            pltpu.VMEM((1, GW), F32),
            pltpu.VMEM((1, GW), F32),
            pltpu.VMEM((2 * width, GW), BF16),
            pltpu.VMEM((3, rows), jnp.int32),
            pltpu.VMEM((3, HEAD_DIM), F32),
            pltpu.VMEM((GROUP_HEADS, NX * rows, HEAD_DIM), BF16),
            pltpu.VMEM((GROUP_HEADS, NX * rows, 1), F32),
            pltpu.VMEM((GROUP_HEADS, NX * rows, 1), F32),
            pltpu.VMEM((GROUP_HEADS, NX * rows, HEAD_DIM), F32),
            pltpu.VMEM((NX, rows + 8, 2 * SIDE), F32),
            pltpu.VMEM((2, NX, rows + 8, 2 * SIDE), F32),
            pltpu.SemaphoreType.DMA((12,)),
            pltpu.SemaphoreType.DMA((n_copies,)),
            pltpu.SemaphoreType.DMA((n_copies,)),
        ],
        compiler_params=pltpu.CompilerParams(
            collective_id=0, has_side_effects=True, vmem_limit_bytes=62 * 1024 * 1024
        ),
        name="stale_attention",
    )(
        q, fk, fv, sk, sv, tk, tv, shift, scale, proj.T, positions, jnp.asarray(lane_frequencies()), count
    )
    return jnp.swapaxes(guided, 1, 2)


def solution(mesh):
    nz = mesh.shape["patch"] // (NX * NC)
    placed = (
        P("cfg", "patch", "rep"),
        P("cfg", "patch", "rep"),
        P("cfg", "patch", "rep"),
        P("cfg", "patch", "rep"),
        P("cfg", "patch", "rep"),
        P("cfg", "rep", None),
        P("cfg", "rep", None),
        P("cfg"),
        P("rep", "patch"),
        P("cfg", None),
        P("cfg", None),
        P(),
    )

    def run(*args):
        return shards(nz, *args)

    return jax.shard_map(
        run, mesh=mesh, in_specs=placed, out_specs=P("cfg", "patch", "rep"), check_vma=False
    )
```

time: 57.2 us -> 49.1 us (0.86)
  local copies, waits for them, and re-layouts: 5.14 us -> 1.32 us
  Pallas kernels: 50.6 us -> 46.9 us
    pallas_call x1, Pallas kernels: 50.6 us -> 46.9 us  [shards(): pl.pallas_call(body, out_shape=jax.ShapeDtypeStruct((1, width, rows), F32...]
    unnamed x23 -> x1, local copies, waits for them, and re-layouts: 4.46 us -> 1.32 us
    pallas_call x1 -> x0, local copies, waits for them, and re-layouts: 0.68 us -> none  [shards(): pl.pallas_call(body, out_shape=jax.ShapeDtypeStruct((1, rows, width), F32...]
where the time goes in v2:
time: 49.1 us; the launch traced here: 48.9 us
  Pallas kernels  46.9 us (96%)
  local copies, waits for them, and re-layouts  1.32 us (3%)
  between operations  0.66 us (1%)
    pallas_call x1, Pallas kernels, shards(): pl.pallas_call(body, out_shape=jax.ShapeDtypeStruct((1, width, rows), F32...  46.9 us
    unnamed x1, local copies, waits for them, and re-layouts  1.32 us

profile of v2, /device:TPU:1, one launch (start us, length us, event | category | flops | bytes accessed | tf_op | source)
XLA Modules:
  0.0 48.9 jit_solution(14910805536617394313)
XLA Ops:
  0.7 46.9 %stale_attention.1 = f32[1,32,40]{2,1,0:T(8,128)} custom-call(bf16[1,40,1536]{2,1,0:T(8,128)(2,1)} %refs_0_.1, bf16[1,40,1536]{2,1,0:T(8,128)(2,1)} %refs_1_.1, bf16[1,40,1536]{2,1,0:T(8,128)(2,1)} %refs_2_.1, bf16[1,40,1536]{2,1,0:T(8,128)(2,1)} %refs_3_.1, bf16[1,40,1536]{2,1,0:T(8,128)(2,1)} %refs_4_.1, bf16[1,256,1536]{2,1,0:T(8,128)(2,1)} %refs_5_.1, ...), custom_call_target="tpu_custom_call" | custom-call | tf_op jit(solution)/shard_map/stale_attention/pallas_call | solution.py:413
  47.6 1.3 %copy.16 = f32[1,40,32]{1,2,0:T(8,128)} copy(f32[1,40,32]{1,2,0:T(8,128)} %bitcast.3) | data formatting | bytes 10240

commit v3 on v2

--- a/solution.py
+++ b/solution.py
@@ -20,6 +20,8 @@
 GW = GROUP_HEADS * HEAD_DIM
 SCALE2 = math.log2(math.e) / math.sqrt(HEAD_DIM)
 SIDE = 64
+PACK = 16
+STEP = 40
 F32 = jnp.float32
 BF16 = jnp.bfloat16
 MESH = pl.DeviceIdType.MESH
@@ -147,6 +149,29 @@
     def columns(group):
         return pl.ds(pl.multiple_of(group * GW, 128), GW)
 
+    barrier = pltpu.get_barrier_semaphore()
+    friends = [at(z, owner(d), core) for d in range(1, NX)] + [up, down, sibling]
+    friends += [across(owner(d)) for d in range(NX)]
+    for friend in friends:
+        pl.semaphore_signal(barrier, inc=1, device_id=friend, device_id_type=MESH)
+    pl.semaphore_wait(barrier, len(friends))
+
+    for name, hbm, buf in (("sk", sk_hbm, kbuf), ("sv", sv_hbm, vbuf)):
+        for d in NEAREST:
+            send(
+                ("in", name, d),
+                hbm.at[0, :, columns(owner(d))],
+                buf.at[0, 0, d],
+                at(z, owner(d), core),
+            )
+
+    def spread(kv, src, buf, d):
+        send(("z", kv, 1, d), src, buf.at[1, 0, d], up)
+        send(("z", kv, nz - 1, d), src, buf.at[nz - 1, 0, d], down)
+
+    spread("k", sk_hbm.at[0, :, columns(x)], kbuf, 0)
+    spread("v", sv_hbm.at[0, :, columns(x)], vbuf, 0)
+
     fetch("pos", pos_hbm, pos_ref)
     fetch("freq", freq_hbm, freq_ref)
     fetch("sk", sk_hbm.at[0, :, columns(x)], kbuf.at[0, 0, 0])
@@ -160,31 +185,13 @@
     fetch("scale", scale_hbm.at[:, columns(x)], scalebuf)
     fetch("proj", proj_hbm.at[:, columns(x)], projbuf)
 
-    barrier = pltpu.get_barrier_semaphore()
-    friends = [at(z, owner(d), core) for d in range(1, NX)] + [up, down, sibling]
-    friends += [across(owner(d)) for d in range(NX)]
-    for friend in friends:
-        pl.semaphore_signal(barrier, inc=1, device_id=friend, device_id_type=MESH)
-    pl.semaphore_wait(barrier, len(friends))
-
-    for name, hbm, buf in (("sk", sk_hbm, kbuf), ("sv", sv_hbm, vbuf)):
+    for name, kv, buf in (("sk", "k", kbuf), ("sv", "v", vbuf)):
         for d in NEAREST:
-            send(
-                ("in", name, d),
-                hbm.at[0, :, columns(owner(d))],
-                buf.at[0, 0, d],
-                at(z, owner(d), core),
-            )
-
-    def spread(kv, buf, d):
-        send(("z", kv, 1, d), buf.at[0, 0, d], buf.at[1, 0, d], up)
-        send(("z", kv, nz - 1, d), buf.at[0, 0, d], buf.at[nz - 1, 0, d], down)
-
-    locals_["sk"].wait()
-    spread("k", kbuf, 0)
-    locals_["sv"].wait()
-    spread("v", vbuf, 0)
-
+            arrived(("in", name, d))
+            spread(kv, buf.at[0, 0, d], buf, d)
+    for kv, buf in (("k", kbuf), ("v", vbuf)):
+        locals_["s" + kv].wait()
+        send(("s", kv, 0), buf.at[0, 0], buf.at[0, 1], sibling)
     at_row = lax.broadcasted_iota(jnp.int32, (rows, rows), 0)
     at_col = lax.broadcasted_iota(jnp.int32, (rows, rows), 1)
     locals_["pos"].wait()
@@ -216,12 +223,6 @@
                 target = ownbuf if d == 0 else sendbuf
                 target[max(d - 1, 0) if d else 0, :, h * HEAD_DIM : (h + 1) * HEAD_DIM] = turned
 
-    for name, kv, buf in (("sk", "k", kbuf), ("sv", "v", vbuf)):
-        for d in NEAREST:
-            arrived(("in", name, d))
-            spread(kv, buf, d)
-    for kv, buf in (("k", kbuf), ("v", vbuf)):
-        send(("s", kv, 0), buf.at[0, 0], buf.at[0, 1], sibling)
     for d in NEAREST:
         send(("in", "q", d), qsend.at[d - 1], qbuf.at[d], at(z, owner(d), core))
     for d in NEAREST:
@@ -248,7 +249,18 @@
         )
 
     def weigh(weights, tile):
-        return jnp.dot(weights.astype(BF16), tile, preferred_element_type=F32)
+        wide = jnp.concatenate([tile, jnp.ones_like(tile)], axis=1)
+        return jnp.dot(weights.astype(BF16), wide, preferred_element_type=F32)
+
+    def largest(score):
+        return jnp.broadcast_to(
+            jnp.max(score, axis=1, keepdims=True), (score.shape[0], HEAD_DIM)
+        )
+
+    def relative(score, high):
+        copies = -(-score.shape[1] // HEAD_DIM)
+        wide = jnp.concatenate([high] * copies, axis=1)[:, : score.shape[1]]
+        return jnp.exp2((score - wide) * SCALE2)
 
     all_rows = NX * rows
 
@@ -275,77 +287,42 @@
                 scores_of(h, stacked(kbuf, h, [(0, 0)])),
             )
             word = jnp.where(live, scores_of(h, tkbuf[:, lanes_of(h)]), -jnp.inf)
-            high = jnp.maximum(
-                jnp.max(own, axis=1, keepdims=True), jnp.max(word, axis=1, keepdims=True)
-            )
-            own = jnp.exp2((own - high) * SCALE2)
-            word = jnp.exp2((word - high) * SCALE2)
+            high = jnp.maximum(largest(own), largest(word))
+            own = relative(own, high)
+            word = relative(word, high)
             top[h] = high
-            total[h] = jnp.sum(own, axis=1, keepdims=True) + jnp.sum(word, axis=1, keepdims=True)
-            acc[h] = (
+            summed = (
                 weigh(jnp.where(same, own, 0.0), stacked(fvbuf, h, [()]))
                 + weigh(jnp.where(same, 0.0, own), stacked(vbuf, h, [(0, 0)]))
                 + weigh(word, tvbuf[:, lanes_of(h)])
             )
-
+            acc[h] = summed[:, :HEAD_DIM]
+            total[h] = summed[:, HEAD_DIM:]
+
+    def absorbed(h, slots):
+        score = scores_of(h, stacked(kbuf, h, slots))
+        old = top[h]
+        high = jnp.maximum(old, largest(score))
+        summed = weigh(relative(score, high), stacked(vbuf, h, slots))
+        rescale = jnp.exp2((old - high) * SCALE2)
+        return (
+            high,
+            total[h] * rescale + summed[:, HEAD_DIM:],
+            acc[h] * rescale + summed[:, :HEAD_DIM],
+        )
 
     def absorb(slots):
         for h in range(GROUP_HEADS):
-            score = scores_of(h, stacked(kbuf, h, slots))
-            old = top[h]
-            high = jnp.maximum(old, jnp.max(score, axis=1, keepdims=True))
-            weights = jnp.exp2((score - high) * SCALE2)
-            rescale = jnp.exp2((old - high) * SCALE2)
-            top[h] = high
-            total[h] = total[h] * rescale + jnp.sum(weights, axis=1, keepdims=True)
-            acc[h] = acc[h] * rescale + weigh(weights, stacked(vbuf, h, slots))
+            top[h], total[h], acc[h] = absorbed(h, slots)
 
     def sibling_arrived(r):
         for kv in ("k", "v"):
             arrived(("s", kv, r))
 
-    pending = [0]
-    for t in range(1, half + 1):
-        if t == half:
-            for r in pending:
-                sibling_arrived(r)
-            absorb([(r, 1) for r in pending])
-            pending = []
-        here = []
-        for kv, buf in (("k", kbuf), ("v", vbuf)):
-            for r, step, device in ((t, 1, up), (nz - t, -1, down)):
-                if t == half and (kv == "k") != (step == 1):
-                    continue
-                if t == 1:
-                    for d in range(NX):
-                        arrived(("z", kv, r, d))
-                else:
-                    arrived(("z", kv, r))
-                following = r + step
-                if t < half and (following != half or (kv == "k") == (step == 1)):
-                    send(("z", kv, following), buf.at[r, 0], buf.at[following, 0], device)
-                if r not in here:
-                    here.append(r)
-            for r in here:
-                send(("s", kv, r), buf.at[r, 0], buf.at[r, 1], sibling)
-        if t == 1:
-            begin()
-        for r in pending:
-            sibling_arrived(r)
-        absorb([(r, 0) for r in here] + [(r, 1) for r in pending])
-        pending = here
-    for r in pending:
-        sibling_arrived(r)
-    absorb([(r, 1) for r in pending])
-
-    for name in ("shift", "scale", "proj"):
-        locals_[name].wait()
+    first = branch == 0
     width = projbuf.shape[0] // 2
-    gap = jnp.zeros((SIDE - width, GW), BF16)
-    channels = jnp.concatenate([projbuf[:width], gap, projbuf[width:], gap], axis=0)
-
-    def project(value, h):
-        tile = channels[:, lanes_of(h)]
+
+    def project(value, tile):
         big = value.astype(BF16)
         small = (value - big.astype(F32)).astype(BF16)
         nt = (((1,), (1,)), ((), ()))
@@ -353,31 +330,104 @@
             big, tile, nt, preferred_element_type=F32
         ) + lax.dot_general(small, tile, nt, preferred_element_type=F32)
 
+    def forward(kv, buf, t):
+        for r, step, device in ((t, 1, up), (nz - t, -1, down)):
+            if t == 1:
+                for d in range(NX):
+                    arrived(("z", kv, r, d))
+            else:
+                arrived(("z", kv, r))
+            following = r + step
+            if following != half or (kv == "k") == (step == 1):
+                send(("z", kv, following), buf.at[r, 0], buf.at[following, 0], device)
+        for r in (t, nz - t):
+            send(("s", kv, r), buf.at[r, 0], buf.at[r, 1], sibling)
+
+    both = (("k", kbuf), ("v", vbuf))
+    backlog = []
+    for t in range(1, half):
+        for kv, buf in both:
+            forward(kv, buf, t)
+            if t == 2 and kv == "k":
+                begin()
+            elif t >= 2:
+                for slot in backlog:
+                    if slot[1] == 1:
+                        sibling_arrived(slot[0])
+                for i in range(0, len(backlog), 4):
+                    absorb(backlog[i : i + 4])
+                backlog = []
+            if kv == "v":
+                backlog += [(r, s) for s in (0, 1) for r in (t, nz - t)]
+                if t == 1:
+                    backlog += [(0, 1)]
+    if half == 2:
+        begin()
+    for name in ("shift", "scale", "proj"):
+        locals_[name].wait()
+    low, high_half = projbuf[:width], projbuf[width:]
+    gap = jnp.zeros((SIDE - width, GW), BF16)
+    channels = jnp.concatenate(
+        [jnp.where(first, low, high_half), gap, jnp.where(first, high_half, low), gap], axis=0
+    )
     gain = 1.0 + scalebuf[...]
-    affine = jnp.concatenate([gain, shiftbuf[...], jnp.zeros((6, GW), F32)], axis=0)
-    affine = sum(project(affine[:, lanes_of(h)], h) for h in range(GROUP_HEADS))
-    attended = [acc[h] / total[h] for h in range(GROUP_HEADS)]
-    mean = sum(jnp.sum(part, axis=1, keepdims=True) for part in attended) / GW
+    affine = project(
+        jnp.concatenate([gain, shiftbuf[...], jnp.zeros((6, GW), F32)], axis=0), channels
+    )
+    early, late = backlog[:2], backlog[2:]
+    absorb(early)
+    for slot in late:
+        sibling_arrived(slot[0])
+    absorb(late)
+    for kv, buf in both:
+        arrived(("z", kv, half))
+        send(("s", kv, half), buf.at[half, 0], buf.at[half, 1], sibling)
+    absorb([(half, 0)])
+    sibling_arrived(half)
+
+    attended = []
+    for h in range(GROUP_HEADS):
+        _, totals, sums = absorbed(h, [(half, 1)])
+        attended.append(sums / totals)
+    mean = jnp.sum(sum(attended), axis=1, keepdims=True) / GW
     attended = [part - mean for part in attended]
-    squares = sum(jnp.sum(part * part, axis=1, keepdims=True) for part in attended)
-    share = sum(project(attended[h] * gain[:, lanes_of(h)], h) for h in range(GROUP_HEADS))
+    squares = jnp.sum(sum(part * part for part in attended), axis=1, keepdims=True)
+    share = sum(
+        project(attended[h] * gain[:, lanes_of(h)], channels[:, lanes_of(h)])
+        for h in range(GROUP_HEADS)
+    )
     lane = lax.rem(lax.broadcasted_iota(jnp.int32, share.shape, 1), SIDE)
     share = jnp.where(lane == width, mean, jnp.where(lane == width + 1, squares, share))
-    for d in range(NX):
-        ysend[d, :rows] = share[d * rows : (d + 1) * rows]
-        ysend[d, rows:] = affine
-    for d in NEAREST:
-        send(("own", d), ysend.at[d], yrecv.at[0, d], at(z, asker(d), core))
-    for d in (0,) + NEAREST:
-        send(("other", d), ysend.at[d], yrecv.at[1, d], across(asker(d)))
-    yrecv[0, 0] = ysend[0]
-    for d in NEAREST:
-        arrived(("own", d))
-    for d in range(NX):
-        arrived(("other", d))
+    slot = lax.broadcasted_iota(jnp.int32, (PACK, HEAD_DIM), 1) // STEP
+
+    def turn(value, shift):
+        return pltpu.roll(value, shift % HEAD_DIM, 1) if shift % HEAD_DIM else value
+
+    for side, d in [(1, 2), (1, 1), (1, 3), (0, 2), (0, 1), (0, 3), (1, 0), (0, 0)]:
+        block = share[d * rows : (d + 1) * rows]
+        strips = [
+            block[:PACK],
+            block[PACK : 2 * PACK],
+            jnp.concatenate([block[2 * PACK :], affine], axis=0),
+        ]
+        strips = [turn(strip, i * STEP - side * SIDE) for i, strip in enumerate(strips)]
+        packed = jnp.where(slot == 0, strips[0], jnp.where(slot == 1, strips[1], strips[2]))
+        if (side, d) == (0, 0):
+            yrecv[0, 0] = packed
+        else:
+            ysend[side, d] = packed
+            if side:
+                send(("other", d), ysend.at[1, d], yrecv.at[1, d], across(asker(d)))
+            else:
+                send(("own", d), ysend.at[0, d], yrecv.at[0, d], at(z, asker(d), core))
 
     def prediction(side):
-        blocks = [yrecv[side, d] for d in range(NX)]
+        blocks = []
+        for d in range(NX):
+            packed = yrecv[side, d]
+            blocks.append(
+                jnp.concatenate([packed, turn(packed, -STEP), turn(packed, -2 * STEP)], axis=0)
+            )
         means = [block[:rows, width : width + 1] for block in blocks]
         middle = sum(means) / NX
         spread_ = sum(block[:rows, width + 1 : width + 2] for block in blocks)
@@ -389,11 +439,15 @@
         )
         return inverse * linear + sum(block[rows + 1 : rows + 2] for block in blocks)
 
-    first = branch == 0
     own_weight = jnp.where(first, 1.0 - GUIDANCE, GUIDANCE)
     other_weight = jnp.where(first, GUIDANCE, 1.0 - GUIDANCE)
-    guided = (own_weight * prediction(0) + other_weight * prediction(1)).T
-    out_ref[0] = jnp.where(first, guided[:width], guided[SIDE : SIDE + width])
+    for d in NEAREST:
+        arrived(("own", d))
+    guided = own_weight * prediction(0)
+    for d in range(NX):
+        arrived(("other", d))
+    guided = (guided + other_weight * prediction(1)).T
+    out_ref[0] = guided[:width]
     for copy in started.values():
         copy.wait_send()
 
@@ -432,11 +486,11 @@
             pltpu.VMEM((3, rows), jnp.int32),
             pltpu.VMEM((3, HEAD_DIM), F32),
             pltpu.VMEM((GROUP_HEADS, NX * rows, HEAD_DIM), BF16),
-            pltpu.VMEM((GROUP_HEADS, NX * rows, 1), F32),
-            pltpu.VMEM((GROUP_HEADS, NX * rows, 1), F32),
             pltpu.VMEM((GROUP_HEADS, NX * rows, HEAD_DIM), F32),
-            pltpu.VMEM((NX, rows + 8, 2 * SIDE), F32),
-            pltpu.VMEM((2, NX, rows + 8, 2 * SIDE), F32),
+            pltpu.VMEM((GROUP_HEADS, NX * rows, HEAD_DIM), F32),
+            pltpu.VMEM((GROUP_HEADS, NX * rows, HEAD_DIM), F32),
+            pltpu.VMEM((2, NX, PACK, HEAD_DIM), F32),
+            pltpu.VMEM((2, NX, PACK, HEAD_DIM), F32),
             pltpu.SemaphoreType.DMA((12,)),
             pltpu.SemaphoreType.DMA((n_copies,)),
             pltpu.SemaphoreType.DMA((n_copies,)),

time: 49.1 us -> 47.2 us (0.961)
  Pallas kernels: 46.9 us -> 45 us
    pallas_call x1, Pallas kernels: 46.9 us -> 45 us  [shards(): pl.pallas_call(body, out_shape=jax.ShapeDtypeStruct((1, width, rows), F32...]
where the time goes in v3:
time: 47.2 us; the launch traced here: 47 us
  Pallas kernels  45 us (95%)
  local copies, waits for them, and re-layouts  1.32 us (3%)
  between operations  0.66 us (1%)
    pallas_call x1, Pallas kernels, shards(): pl.pallas_call(body, out_shape=jax.ShapeDtypeStruct((1, width, rows), F32...  45 us
    unnamed x1, local copies, waits for them, and re-layouts  1.32 us

profile of v3, /device:TPU:1, one launch (start us, length us, event | category | flops | bytes accessed | tf_op | source)
XLA Modules:
  0.0 47.0 jit_solution(15074843304154451351)
XLA Ops:
  0.7 45.0 %stale_attention.1 = f32[1,32,40]{2,1,0:T(8,128)} custom-call(bf16[1,40,1536]{2,1,0:T(8,128)(2,1)} %refs_0_.1, bf16[1,40,1536]{2,1,0:T(8,128)(2,1)} %refs_1_.1, bf16[1,40,1536]{2,1,0:T(8,128)(2,1)} %refs_2_.1, bf16[1,40,1536]{2,1,0:T(8,128)(2,1)} %refs_3_.1, bf16[1,40,1536]{2,1,0:T(8,128)(2,1)} %refs_4_.1, bf16[1,256,1536]{2,1,0:T(8,128)(2,1)} %refs_5_.1, ...), custom_call_target="tpu_custom_call" | custom-call | tf_op jit(solution)/shard_map/stale_attention/pallas_call | solution.py:467
  45.7 1.3 %copy.16 = f32[1,40,32]{1,2,0:T(8,128)} copy(f32[1,40,32]{1,2,0:T(8,128)} %bitcast.3) | data formatting | bytes 10240

commit v4 on v3

--- a/solution.py
+++ b/solution.py
@@ -1,3 +1,4 @@
+import functools
 import math
 
 import jax
@@ -38,6 +39,10 @@
         rows[axis, start : start + extent] = np.repeat(frequency, 2)
         start += extent
     return rows
+
+
+def turn(value, shift):
+    return pltpu.roll(value, shift % HEAD_DIM, 1) if shift % HEAD_DIM else value
 
 
 def copy_keys(nz):
@@ -71,7 +76,7 @@
     pos_hbm,
     freq_hbm,
     cnt_ref,
-    out_ref,
+    yrecv,
     raw,
     qsend,
     fksend,
@@ -92,7 +97,6 @@
     total,
     acc,
     ysend,
-    yrecv,
     local_sem,
     send_sem,
     recv_sem,
@@ -122,6 +126,7 @@
         return {"cfg": 1 - branch, **at(z, xx, core)}
 
     started = {}
+    drained = set()
 
     def send(key, src, dst, device):
         i = keys[key]
@@ -138,6 +143,11 @@
 
     def arrived(key):
         started[key].wait_recv()
+
+    def drain(keep=()):
+        for key in [key for key in started if key not in drained and key not in keep]:
+            started[key].wait_send()
+            drained.add(key)
 
     locals_ = {}
 
@@ -379,6 +389,7 @@
     for slot in late:
         sibling_arrived(slot[0])
     absorb(late)
+    drain([("z", "k", half), ("z", "v", half)])
     for kv, buf in both:
         arrived(("z", kv, half))
         send(("s", kv, half), buf.at[half, 0], buf.at[half, 1], sibling)
@@ -400,9 +411,6 @@
     share = jnp.where(lane == width, mean, jnp.where(lane == width + 1, squares, share))
     slot = lax.broadcasted_iota(jnp.int32, (PACK, HEAD_DIM), 1) // STEP
 
-    def turn(value, shift):
-        return pltpu.roll(value, shift % HEAD_DIM, 1) if shift % HEAD_DIM else value
-
     for side, d in [(1, 2), (1, 1), (1, 3), (0, 2), (0, 1), (0, 3), (1, 0), (0, 0)]:
         block = share[d * rows : (d + 1) * rows]
         strips = [
@@ -412,15 +420,24 @@
         ]
         strips = [turn(strip, i * STEP - side * SIDE) for i, strip in enumerate(strips)]
         packed = jnp.where(slot == 0, strips[0], jnp.where(slot == 1, strips[1], strips[2]))
+        ysend[side, d] = packed
         if (side, d) == (0, 0):
-            yrecv[0, 0] = packed
+            fetch("self", ysend.at[0, 0], yrecv.at[0, 0])
         else:
-            ysend[side, d] = packed
             if side:
                 send(("other", d), ysend.at[1, d], yrecv.at[1, d], across(asker(d)))
             else:
                 send(("own", d), ysend.at[0, d], yrecv.at[0, d], at(z, asker(d), core))
 
+    drain()
+    locals_["self"].wait()
+    for d in NEAREST:
+        arrived(("own", d))
+    for d in range(NX):
+        arrived(("other", d))
+
+
+def combine(rows, width, yrecv, out_ref):
     def prediction(side):
         blocks = []
         for d in range(NX):
@@ -439,17 +456,11 @@
         )
         return inverse * linear + sum(block[rows + 1 : rows + 2] for block in blocks)
 
+    first = lax.axis_index("cfg") == 0
     own_weight = jnp.where(first, 1.0 - GUIDANCE, GUIDANCE)
     other_weight = jnp.where(first, GUIDANCE, 1.0 - GUIDANCE)
-    for d in NEAREST:
-        arrived(("own", d))
-    guided = own_weight * prediction(0)
-    for d in range(NX):
-        arrived(("other", d))
-    guided = (guided + other_weight * prediction(1)).T
+    guided = (own_weight * prediction(0) + other_weight * prediction(1)).T
     out_ref[0] = guided[:width]
-    for copy in started.values():
-        copy.wait_send()
 
 
 def shards(nz, *args):
@@ -464,11 +475,11 @@
     def body(*refs):
         kernel(nz, rows, *refs)
 
-    guided = pl.pallas_call(
+    returned = pl.pallas_call(
         body,
-        out_shape=jax.ShapeDtypeStruct((1, width, rows), F32),
+        out_shape=jax.ShapeDtypeStruct((2, NX, PACK, HEAD_DIM), F32),
         in_specs=[anywhere] * 12 + [pl.BlockSpec(memory_space=pltpu.SMEM)],
-        out_specs=in_vmem,
+        out_specs=anywhere,
         scratch_shapes=[
             pltpu.VMEM((2, rows, features), BF16),
             pltpu.VMEM((NX - 1, rows, GW), BF16),
@@ -490,8 +501,7 @@
             pltpu.VMEM((GROUP_HEADS, NX * rows, HEAD_DIM), F32),
             pltpu.VMEM((GROUP_HEADS, NX * rows, HEAD_DIM), F32),
             pltpu.VMEM((2, NX, PACK, HEAD_DIM), F32),
-            pltpu.VMEM((2, NX, PACK, HEAD_DIM), F32),
-            pltpu.SemaphoreType.DMA((12,)),
+            pltpu.SemaphoreType.DMA((13,)),
             pltpu.SemaphoreType.DMA((n_copies,)),
             pltpu.SemaphoreType.DMA((n_copies,)),
         ],
@@ -502,6 +512,13 @@
     )(
         q, fk, fv, sk, sv, tk, tv, shift, scale, proj.T, positions, jnp.asarray(lane_frequencies()), count
     )
+    guided = pl.pallas_call(
+        functools.partial(combine, rows, width),
+        out_shape=jax.ShapeDtypeStruct((1, width, rows), F32),
+        in_specs=[in_vmem],
+        out_specs=in_vmem,
+        name="guided_output",
+    )(returned)
     return jnp.swapaxes(guided, 1, 2)
 
 

time: 47.2 us -> 46.5 us (0.985)
  local copies, waits for them, and re-layouts: 1.32 us -> 0 us
  Pallas kernels: 45 us -> 45.7 us
    unnamed x1 -> x0, local copies, waits for them, and re-layouts: 1.32 us -> none
    pallas_call x1 -> x2, Pallas kernels: 45 us -> 45.7 us  [the longest x1 43.9 us: shards(): pl.pallas_call(body, out_shape=jax.ShapeDtypeStruct((2, NX, PACK, HEAD_DI...]
where the time goes in v4:
time: 46.5 us; the launch traced here: 46.4 us
  Pallas kernels  45.7 us (98%)
  between operations  0.66 us (1%)
    pallas_call x1, Pallas kernels, shards(): pl.pallas_call(body, out_shape=jax.ShapeDtypeStruct((2, NX, PACK, HEAD_DI...  43.9 us
    pallas_call x1, Pallas kernels, shards(): pl.pallas_call(functools.partial(combine, rows, width), out_shape=jax.Sha...  1.77 us

profile of v4, /device:TPU:1, one launch (start us, length us, event | category | flops | bytes accessed | tf_op | source)
XLA Modules:
  0.0 46.4 jit_solution(1723314734958506749)
XLA Ops:
  0.7 43.9 %stale_attention.1.yrecv = f32[2,4,16,128]{3,2,1,0:T(8,128)} custom-call(bf16[1,40,1536]{2,1,0:T(8,128)(2,1)} %refs_0_.1, bf16[1,40,1536]{2,1,0:T(8,128)(2,1)} %refs_1_.1, bf16[1,40,1536]{2,1,0:T(8,128)(2,1)} %refs_2_.1, bf16[1,40,1536]{2,1,0:T(8,128)(2,1)} %refs_3_.1, bf16[1,40,1536]{2,1,0:T(8,128)(2,1)} %refs_4_.1, bf16[1,256,1536]{2,1,0:T(8,128)(2,1)} %refs_5_.1, ...), custom_call_target="tpu_custom_call" | custom-call | tf_op jit(solution)/shard_map/stale_attention/pallas_call | solution.py:478
  44.6 1.8 %guided_output.1 = f32[1,32,40]{2,1,0:T(8,128)} custom-call(f32[2,4,16,128]{3,2,1,0:T(8,128)} %stale_attention.1.yrecv), custom_call_target="tpu_custom_call" | custom-call | tf_op jit(solution)/shard_map/guided_output/pallas_call | solution.py:515

commit v5 on v4

--- a/solution.py
+++ b/solution.py
@@ -161,7 +161,7 @@
 
     barrier = pltpu.get_barrier_semaphore()
     friends = [at(z, owner(d), core) for d in range(1, NX)] + [up, down, sibling]
-    friends += [across(owner(d)) for d in range(NX)]
+    friends += [across(x)]
     for friend in friends:
         pl.semaphore_signal(barrier, inc=1, device_id=friend, device_id_type=MESH)
     pl.semaphore_wait(barrier, len(friends))

time: 46.5 us -> 46.4 us (level)
  no operation moved by 1% of the time
where the time goes in v5:
time: 46.4 us; the launch traced here: 46.3 us
  Pallas kernels  45.6 us (98%)
  between operations  0.66 us (1%)
    pallas_call x1, Pallas kernels, shards(): pl.pallas_call(body, out_shape=jax.ShapeDtypeStruct((2, NX, PACK, HEAD_DI...  43.8 us
    pallas_call x1, Pallas kernels, shards(): pl.pallas_call(functools.partial(combine, rows, width), out_shape=jax.Sha...  1.77 us

profile of v5, /device:TPU:1, one launch (start us, length us, event | category | flops | bytes accessed | tf_op | source)
XLA Modules:
  0.0 46.3 jit_solution(12593098882735751883)
XLA Ops:
  0.7 43.8 %stale_attention.1.yrecv = f32[2,4,16,128]{3,2,1,0:T(8,128)} custom-call(bf16[1,40,1536]{2,1,0:T(8,128)(2,1)} %refs_0_.1, bf16[1,40,1536]{2,1,0:T(8,128)(2,1)} %refs_1_.1, bf16[1,40,1536]{2,1,0:T(8,128)(2,1)} %refs_2_.1, bf16[1,40,1536]{2,1,0:T(8,128)(2,1)} %refs_3_.1, bf16[1,40,1536]{2,1,0:T(8,128)(2,1)} %refs_4_.1, bf16[1,256,1536]{2,1,0:T(8,128)(2,1)} %refs_5_.1, ...), custom_call_target="tpu_custom_call" | custom-call | tf_op jit(solution)/shard_map/stale_attention/pallas_call | solution.py:478
  44.5 1.8 %guided_output.1 = f32[1,32,40]{2,1,0:T(8,128)} custom-call(f32[2,4,16,128]{3,2,1,0:T(8,128)} %stale_attention.1.yrecv), custom_call_target="tpu_custom_call" | custom-call | tf_op jit(solution)/shard_map/guided_output/pallas_call | solution.py:515

commit v6 on v5

--- a/solution.py
+++ b/solution.py
@@ -52,6 +52,9 @@
             keys += [("z", kv, 1, d), ("z", kv, nz - 1, d)]
         keys.append(("s", kv, 0))
         for r in range(1, nz):
+            if r == nz // 2:
+                keys += [(way, kv, r, part) for way in ("s", "z") for part in (0, 1)]
+                continue
             keys.append(("s", kv, r))
             if r not in (1, nz - 1):
                 keys.append(("z", kv, r))
@@ -348,8 +351,13 @@
             else:
                 arrived(("z", kv, r))
             following = r + step
-            if following != half or (kv == "k") == (step == 1):
+            if following != half:
                 send(("z", kv, following), buf.at[r, 0], buf.at[following, 0], device)
+            elif (kv == "k") == (step == 1):
+                for part in (0, 1):
+                    some = pl.ds(part * NX // 2, NX // 2)
+                    source, target = buf.at[r, 0, some], buf.at[half, 0, some]
+                    send(("z", kv, half, part), source, target, device)
         for r in (t, nz - t):
             send(("s", kv, r), buf.at[r, 0], buf.at[r, 1], sibling)
 
@@ -389,12 +397,16 @@
     for slot in late:
         sibling_arrived(slot[0])
     absorb(late)
-    drain([("z", "k", half), ("z", "v", half)])
-    for kv, buf in both:
-        arrived(("z", kv, half))
-        send(("s", kv, half), buf.at[half, 0], buf.at[half, 1], sibling)
+    drain([("z", kv, half, part) for kv in ("k", "v") for part in (0, 1)])
+    for part in (0, 1):
+        some = pl.ds(part * NX // 2, NX // 2)
+        for kv, buf in both:
+            arrived(("z", kv, half, part))
+            send(("s", kv, half, part), buf.at[half, 0, some], buf.at[half, 1, some], sibling)
     absorb([(half, 0)])
-    sibling_arrived(half)
+    for part in (0, 1):
+        for kv in ("k", "v"):
+            arrived(("s", kv, half, part))
 
     attended = []
     for h in range(GROUP_HEADS):

time: 46.4 us -> 46.6 us (level)
  no operation moved by 1% of the time
where the time goes in v6:
time: 46.6 us; the launch traced here: 46.4 us
  Pallas kernels  45.8 us (98%)
  between operations  0.66 us (1%)
    pallas_call x1, Pallas kernels, shards(): pl.pallas_call(body, out_shape=jax.ShapeDtypeStruct((2, NX, PACK, HEAD_DI...  44 us
    pallas_call x1, Pallas kernels, shards(): pl.pallas_call(functools.partial(combine, rows, width), out_shape=jax.Sha...  1.77 us

profile of v6, /device:TPU:1, one launch (start us, length us, event | category | flops | bytes accessed | tf_op | source)
XLA Modules:
  0.0 46.4 jit_solution(16893040912329013233)
XLA Ops:
  0.7 44.0 %stale_attention.1.yrecv = f32[2,4,16,128]{3,2,1,0:T(8,128)} custom-call(bf16[1,40,1536]{2,1,0:T(8,128)(2,1)} %refs_0_.1, bf16[1,40,1536]{2,1,0:T(8,128)(2,1)} %refs_1_.1, bf16[1,40,1536]{2,1,0:T(8,128)(2,1)} %refs_2_.1, bf16[1,40,1536]{2,1,0:T(8,128)(2,1)} %refs_3_.1, bf16[1,40,1536]{2,1,0:T(8,128)(2,1)} %refs_4_.1, bf16[1,256,1536]{2,1,0:T(8,128)(2,1)} %refs_5_.1, ...), custom_call_target="tpu_custom_call" | custom-call | tf_op jit(solution)/shard_map/stale_attention/pallas_call | solution.py:490
  44.7 1.8 %guided_output.1 = f32[1,32,40]{2,1,0:T(8,128)} custom-call(f32[2,4,16,128]{3,2,1,0:T(8,128)} %stale_attention.1.yrecv), custom_call_target="tpu_custom_call" | custom-call | tf_op jit(solution)/shard_map/guided_output/pallas_call | solution.py:527
